TPU v7x, 128 devices: a whole 4x4x4 slice. The times are simulated.
128 devices in a mesh: dp: 16 (over z, y_lo, core), tensor: 8 (over x, y_hi).
Axes of the slice: x: 4, y: 4 (y_hi: 2, y_lo: 2; y = y_hi * 2 + y_lo), z: 4, core: 2. Of those that a mesh axis runs over, the one named last changes fastest.
Arguments:
- activations: bfloat16 [24576, 14336], P('dp', 'tensor'), as said below
- out_grads: bfloat16 [24576, 4096], P('dp', 'tensor'), as said below
- noise: float32 [4096, 14336], P('dp', 'tensor'), may hold values from -96 to 96
Outputs:
- noisy_grad: float32 [4096, 14336], P('dp', 'tensor')
Inputs may be any that keep to these rules, and one draw needn't show every extreme that they name: `activations`: Finite; each row is one token's hidden units. `out_grads`: Finite; each row is one token's output gradient.
All inputs are finite; a program needn't handle non-finite values.
Results may differ from a plain program's by a relative error of at most 0.0003.
Values may be sent and summed in bfloat16 or wider, within the bound.
A program may use at most 128 MiB of HBM per device.

v0:
```python
import jax
import jax.numpy as jnp
from jax import lax
from jax.sharding import PartitionSpec as P

D = 4096
FF = 14336
SEQ = 256


def per_device(activations, out_grads, noise):
    local_tokens = activations.shape[0]
    count = local_tokens // SEQ
    hidden_local = activations.shape[1]
    full_grads = lax.all_gather(out_grads, "tensor", axis=1, tiled=True)
    acts = activations.reshape(count, SEQ, hidden_local)
    act_gram = jnp.einsum("bsf,btf->bst", acts, acts, preferred_element_type=jnp.float32)
    shard_grads = out_grads.reshape(count, SEQ, out_grads.shape[1])
    grad_gram = jnp.einsum(
        "bsd,btd->bst", shard_grads, shard_grads, preferred_element_type=jnp.float32
    )
    act_gram, grad_gram = lax.psum((act_gram, grad_gram), "tensor")
    sq_norm = jnp.sum(act_gram * grad_gram, axis=(1, 2))
    bound = 0.15 * jnp.sqrt(jnp.float32(SEQ) * FF * D)
    factor = jnp.minimum(1.0, bound / jnp.sqrt(sq_norm + 1e-06))
    rows = D // lax.axis_size("dp")
    columns = full_grads.reshape(count, SEQ, rows * lax.axis_size("dp"))
    each = jnp.einsum("bsd,bsf->bdf", columns, acts, preferred_element_type=jnp.float32)
    summed = lax.psum_scatter(
        jnp.sum(each * factor[:, None, None], axis=0), "dp", scatter_dimension=0, tiled=True
    )
    total = count * lax.axis_size("dp")
    return (summed + noise) / total


def solution(mesh):
    return jax.shard_map(
        per_device,
        mesh=mesh,
        in_specs=(P("dp", "tensor"), P("dp", "tensor"), P("dp", "tensor")),
        out_specs=P("dp", "tensor"),
        check_vma=False,
    )
```

profile of v0, /device:TPU:0, one launch (start us, length us, event | category | flops | bytes accessed | tf_op | source)
XLA Modules:
  0.0 695.3 jit_solution(7917249834134802242)
XLA Ops:
  6.5 0.0 all-reduce.3.cloned.1.call-start
  6.5 0.0 copy-start
  6.5 7.1 %fusion = f32[6,256,256]{2,1,0:T(8,128)} fusion(bf16[6,256,1792]{2,1,0:T(8,128)(2,1)} %bitcast.11), kind=kOutput, calls=%fused_computation.4 | convolution fusion | flops 1409286144 | bytes 7077888 | tf_op jit(solution)/shard_map/bsf,btf->bst/dot_general | solution.py:17
  13.6 0.0 copy-done
  13.6 1.7 fusion.1
  15.4 0.0 all-reduce.3.cloned.1.call-update
  15.4 0.0 all-gather.2.cloned.1.call-start
  15.4 0.7 all-gather.2.cloned.1.call-update
  16.1 0.0 reduce-scatter.2.cloned.1.call-start
  16.2 149.0 %all-reduce.3.cloned.1.call-done = (f32[6,256,256]{2,1,0:T(8,128)}, f32[6,256,256]{2,1,0:T(8,128)}) async-done(((f32[6,256,256]{2,1,0:T(8,128)}, f32[6,256,256]{2,1,0:T(8,128)}), (f32[6,256,256]{2,1,0:T(8,128)}, f32[6,256,256]{2,1,0:T(8,128)})) %all-reduce.3.cloned.1.call-update) | async-done | bytes 3145744 | tf_op jit(solution)/shard_map/psum | solution.py:22
  165.2 2.1 multiply_reduce_fusion.1
  167.4 164.8 %all-gather.2.cloned.1.call-done = bf16[1536,4096]{1,0:T(8,128)(2,1)} async-done(((bf16[1536,512]{1,0:T(8,128)(2,1)}), bf16[1536,4096]{1,0:T(8,128)(2,1)}) %all-gather.2.cloned.1.call-update) | async-done | bytes 12582928 | tf_op jit(solution)/shard_map/all_gather | solution.py:15
  332.2 45.3 %multiply_reduce_fusion = f32[4096,1792]{1,0:T(8,128)} fusion(f32[6]{0:T(128)S(1)} %multiply_minimum_fusion, bf16[6,256,4096]{2,1,0:T(8,128)(2,1)} %bitcast.10, bf16[6,256,1792]{2,1,0:T(8,128)(2,1)} %bitcast.12), kind=kOutput, calls=%fused_computation | convolution fusion | flops 22629318656 | bytes 47448088 | tf_op jit(solution)/shard_map/bsd,bsf->bdf/dot_general | solution.py:28
  377.4 0.0 copy-start.1
  377.4 0.0 reduce-scatter.2.cloned.1.call-update
  377.4 308.4 %reduce-scatter.2.cloned.1.call-done = f32[256,1792]{1,0:T(8,128)} async-done(((f32[4096,1792]{1,0:T(8,128)}), f32[256,1792]{1,0:T(8,128)}) %reduce-scatter.2.cloned.1.call-update) | async-done | bytes 1835024 | tf_op jit(solution)/shard_map/reduce_scatter | solution.py:29
  685.8 0.0 copy-done.1
  685.8 2.9 add_multiply_fusion
  (1 shorter events, 0.0 us)
Async XLA Ops:
  6.5 158.7 %all-reduce.3.cloned.1.call-start = ((), (), s32[]{:S(2)}) async-start(), calls=%async_computation.3 | async-start | bytes 6291456 | tf_op jit(solution)/shard_map/psum | solution.py:22
  6.5 7.1 %copy-start = (bf16[1536,512]{1,0:T(8,128)(2,1)S(1)}, bf16[1536,512]{1,0:T(8,128)(2,1)}, u32[]{:S(2)}) copy-start(bf16[1536,512]{1,0:T(8,128)(2,1)} %param.4) | copy-start | bytes 4718596
  15.4 316.8 %all-gather.2.cloned.1.call-start = ((), (), s32[]{:S(2)}) async-start(), calls=%async_computation.1 | async-start | bytes 14155776 | tf_op jit(solution)/shard_map/all_gather | solution.py:15
  16.1 669.7 %reduce-scatter.2.cloned.1.call-start = ((), (), s32[]{:S(2)}) async-start(), calls=%async_computation.2 | async-start | bytes 31195136 | tf_op jit(solution)/shard_map/reduce_scatter | solution.py:29
  377.4 308.4 %copy-start.1 = (f32[256,1792]{1,0:T(8,128)S(1)}, f32[256,1792]{1,0:T(8,128)}, u32[]{:S(2)}) copy-start(f32[256,1792]{1,0:T(8,128)} %param.5) | copy-start | bytes 5505028
Sparse Core Ops, SparseCore 0:
  15.5 149.6 all-reduce.2
  167.4 164.6 all-gather.1
  377.6 308.2 reduce-scatter.1
where the time goes:
time: 695 us
  waiting for transfers between devices  623 us (90%)
  matrix products  54.1 us (8%)
  between operations  13.1 us (2%)
    reduce_scatter x1, waiting for transfers between devices, per_device(): lax.psum_scatter(jnp.sum(each * factor[:, None, None], axis=0), 'dp', sca...  308 us
    all_gather x1, waiting for transfers between devices, per_device(): full_grads = lax.all_gather(out_grads, 'tensor', axis=1, tiled=True)  165 us
    psum x1, waiting for transfers between devices, per_device(): act_gram, grad_gram = lax.psum((act_gram, grad_gram), 'tensor')  149 us
    dot_general x1, matrix products, per_device(): jnp.einsum('bsd,bsf->bdf', columns, acts, preferred_element_type=jnp.floa...  45.3 us
  transfers between devices with their start and end apart: 3, of which 3 were waited for; matrix products, arithmetic and copies ran while one was open for 0% of the time, Pallas kernels for 0%

commit v1 on v0

v1 whole, which is shorter than its diff:
```python
import functools

import jax
import jax.numpy as jnp
from jax import lax
from jax.experimental import pallas as pl
from jax.experimental.pallas import tpu as pltpu
from jax.sharding import PartitionSpec as P

MESH = pl.DeviceIdType.MESH
F32 = jnp.float32
BF16 = jnp.bfloat16
D = 4096
FF = 14336
SEQ = 256
EX = 6
TOK = EX * SEQ
FL = 1792
DL = 512
PH = 8
RW = 32
SLOTS = 4
GROWS = EX * 32 + 8
COUNT = 96
LANES = 128


def kernel(
    act, g, out,
    H, gin, gT, Gb, GS, GR, SQm, SQ, FAC, Pb, ZR, YR, OS,
    hsem, gsem, hx, gx, gl, gramS, gramR, sqS, sqR, facx, gsnd, grcv, gy, zsnd, zrcv, yrcv, osem,
):
    dp = lax.axis_index("dp")
    t = lax.axis_index("tensor")
    z, yl, c = dp // 4, (dp // 2) % 2, dp % 2
    x, yh = t // 2, t % 2
    oc = 1 - c
    sib = (z * 4 + yl * 2 + oc, t)
    xp, xm = (x + 1) % 4, (x + 3) % 4
    right = (dp, xp * 2 + yh)
    left = (dp, xm * 2 + yh)
    ypeer = (dp, x * 2 + 1 - yh)
    zp, zm, zo = (z + 1) % 4, (z + 3) % 4, (z + 2) % 4
    up = (zp * 4 + yl * 2 + c, t)
    down = (zm * 4 + yl * 2 + c, t)
    ylo = (z * 4 + (1 - yl) * 2 + c, t)

    def remote(src, dst, ssem, rsem, dev):
        return pltpu.make_async_remote_copy(
            src_ref=src, dst_ref=dst, send_sem=ssem, recv_sem=rsem, device_id=dev, device_id_type=MESH
        )

    g_in = pltpu.make_async_copy(g, gin, gsem)
    g_in.start()

    def h_in(e):
        rows = pl.ds(e * SEQ, SEQ)
        return pltpu.make_async_copy(act.at[rows], H.at[c, rows], hsem.at[e])

    for e in range(EX):
        h_in(e).start()

    barrier = pltpu.get_barrier_semaphore()
    partners = [(dp, (t + j) % 8) for j in range(1, 8)] + [sib, up, down, ylo]
    for dev in partners:
        pl.semaphore_signal(barrier, inc=1, device_id=dev, device_id_type=MESH)
    pl.semaphore_wait(barrier, len(partners))

    def shard_copy(k, owner, ssem, rsem, dev):
        return remote(Gb.at[k, owner], Gb.at[k, owner], ssem, rsem, dev)

    def own_y(k):
        return shard_copy(k, t, gsnd.at[k, 0], gy.at[k], ypeer)

    def own_x(k, d):
        return shard_copy(k, t, gsnd.at[k, 1 + d], grcv.at[k, d, 0], right if d == 0 else left)

    def peer_x(k, d):
        return shard_copy(k, x * 2 + 1 - yh, gsnd.at[k, 3 + d], grcv.at[k, d, 1], right if d == 0 else left)

    def fwd_x(k, d):
        owner = xm * 2 if d == 0 else xp * 2 + 1
        return shard_copy(k, owner, gsnd.at[k, 5 + d], grcv.at[k, d, 2], right if d == 0 else left)

    def wait_shard(k, d, kind):
        shard_copy(k, t, gsnd.at[k, 0], grcv.at[k, d, kind], ypeer).wait_recv()

    def start_own_x(k):
        own_x(k, 0).start()
        own_x(k, 1).start()

    def start_peer_x(k):
        own_y(k).wait_recv()
        peer_x(k, 0).start()
        peer_x(k, 1).start()

    def start_fwd_x(k):
        wait_shard(k, 0, yh)
        fwd_x(k, 0).start()
        wait_shard(k, 1, 1 - yh)
        fwd_x(k, 1).start()

    def wait_rest(k):
        wait_shard(k, 0, 1 - yh)
        wait_shard(k, 1, yh)
        wait_shard(k, 0, 2)
        wait_shard(k, 1, 2)

    g_in.wait()
    for e in range(EX):
        tr = gin[e * SEQ : (e + 1) * SEQ, :].T
        gT[:, :, :, e * SEQ : (e + 1) * SEQ] = tr.reshape(2, PH, RW, SEQ)
    g_local = pltpu.make_async_copy(gT.at[c], Gb.at[:, t, c], gl)
    g_sib = remote(gT.at[oc], Gb.at[:, t, c], gx.at[0], gx.at[1], sib)
    g_local.start()
    g_sib.start()
    for e in range(EX):
        h_in(e).wait()
    h_sib = remote(H.at[c], H.at[c], hx.at[0], hx.at[1], sib)
    h_sib.start()
    g_local.wait()
    g_sib.wait()
    for k in range(2):
        own_y(k).start()
    start_own_x(0)

    i0 = lax.broadcasted_iota(jnp.int32, (LANES, LANES), 0)
    i1 = lax.broadcasted_iota(jnp.int32, (LANES, LANES), 1)
    e8 = lax.broadcasted_iota(jnp.int32, (8, LANES), 0)
    nt = (((1,), (1,)), ((), ()))

    def gram(e, diags):
        rows = pl.ds(pl.multiple_of(e * SEQ, SEQ), SEQ)
        result = []
        for m in range(2):
            r = H[c, rows, :] if m == 0 else gin[rows, :]
            a = lax.dot_general(r, r, nt, preferred_element_type=F32)
            packed = jnp.where(i0 >= i1, a[:LANES, :LANES], a[LANES:, LANES:])
            below = a[LANES:, :LANES]
            for r8 in range(8):
                part = packed if r8 < 4 else below
                lo = (r8 % 4) * 32
                GS[r8, pl.ds(pl.multiple_of(m * GROWS + e * 32, 8), 32), :] = part[lo : lo + 32]
            diag = jnp.sum(jnp.where(i0 == i1, a[LANES:, LANES:], 0.0), axis=0, keepdims=True)
            result.append(jnp.where(e8 == e, diag, diags[m]))
        return tuple(result)

    zero8 = jnp.zeros((8, LANES), F32)
    diags = lax.fori_loop(0, EX, gram, (zero8, zero8))
    for m in range(2):
        for r8 in range(8):
            GS[r8, m * GROWS + EX * 32 : (m + 1) * GROWS, :] = diags[m]

    def gram_copy(j):
        peer = (t + j) % 8
        return remote(GS.at[peer], GR.at[t], gramS.at[j], gramR.at[j], (dp, peer))

    for j in range(1, 8):
        gram_copy(j).start()
    GR[t] = GS[t]
    start_peer_x(0)
    own_y(2).start()
    start_own_x(1)
    start_fwd_x(0)
    start_peer_x(1)
    for j in range(1, 8):
        gram_copy(j).wait_recv()

    total = GR[0]
    for s in range(1, 8):
        total = total + GR[s]
    prod = total[:GROWS] * total[GROWS:]
    r32 = lax.broadcasted_iota(jnp.int32, (32, LANES), 0)
    l32 = lax.broadcasted_iota(jnp.int32, (32, LANES), 1)
    weight = jnp.where(l32 == r32 + t * 32, 1.0, 2.0)
    l8 = lax.broadcasted_iota(jnp.int32, (8, LANES), 1)
    mine = jnp.where(l8 // 16 == t, prod[EX * 32 :], 0.0)
    for e in range(EX):
        part = jnp.sum(prod[e * 32 : (e + 1) * 32] * weight, axis=0, keepdims=True)
        mine = mine + jnp.where(e8 == e, part, 0.0)
    SQm[...] = mine
    SQ[t] = mine

    def sq_copy(j):
        peer = (t + j) % 8
        return remote(SQm, SQ.at[t], sqS.at[j], sqR.at[j], (dp, peer))

    for j in range(1, 8):
        sq_copy(j).start()
    for j in range(1, 8):
        sq_copy(j).wait_recv()
    sq = SQ[0]
    for s in range(1, 8):
        sq = sq + SQ[s]
    sq = jnp.sum(sq, axis=1, keepdims=True)
    bound = jnp.float32(0.15) * jnp.sqrt(jnp.float32(SEQ) * FF * D)
    factor = jnp.minimum(1.0, bound / jnp.sqrt(jnp.maximum(sq, 0.0) + 1e-06))
    FAC[c] = jnp.broadcast_to(factor, (8, 256))
    fac_sib = remote(FAC.at[c], FAC.at[c], facx.at[0], facx.at[1], sib)
    fac_sib.start()
    h_sib.wait()
    fac_sib.wait()
    for j in range(1, 8):
        gram_copy(j).wait_send()
        sq_copy(j).wait_send()

    def compute(k, s):
        def block(n, carry):
            cols = pl.ds(pl.multiple_of(n * 256, 256), 256)
            acc = None
            for e in range(2 * EX):
                cs, j = divmod(e, EX)
                lhs = Gb[k, :, cs, :, j * SEQ : (j + 1) * SEQ].reshape(8 * RW, SEQ)
                rhs = H[cs, j * SEQ : (j + 1) * SEQ, cols]
                d = jnp.dot(lhs, rhs, preferred_element_type=F32) * FAC[cs, j : j + 1, :]
                acc = d if acc is None else acc + d
            Pb[s, :, :, :, cols] = acc.reshape(4, 2, RW, 256)
            return carry

        lax.fori_loop(0, FL // 256, block, 0)

    def z_copy(k, d, kind):
        s = k % SLOTS
        if kind == 0:
            src = Pb.at[s, zo, d]
        elif kind == 1:
            src = Pb.at[s, zp, 1] if d == 0 else Pb.at[s, zm, 0]
        else:
            src = Pb.at[s, zp, 0] if d == 0 else Pb.at[s, zm, 1]
        return remote(src, ZR.at[k, d, kind], zsnd.at[s, 2 * kind + d], zrcv.at[k, d, kind], up if d == 0 else down)

    def y_copy(k):
        s = k % SLOTS
        return remote(Pb.at[s, z, 1 - yl], YR.at[k], zsnd.at[s, 6], yrcv.at[k], ylo)

    def out_copy(k):
        return pltpu.make_async_copy(OS.at[k], out.at[pl.ds(pl.multiple_of(k * RW, RW), RW)], osem.at[k])

    def send_first(k):
        for kind in range(2):
            for d in range(2):
                z_copy(k, d, kind).start()

    def relay(k):
        s = k % SLOTS
        for d in range(2):
            z_copy(k, d, 0).wait_recv()
            dest = (zp, 0) if d == 0 else (zm, 1)
            Pb[s, dest[0], dest[1]] = Pb[s, dest[0], dest[1]] + ZR[k, d, 0]
            z_copy(k, d, 2).start()

    def last(k):
        s = k % SLOTS
        for kind in (1, 2):
            for d in range(2):
                z_copy(k, d, kind).wait_recv()
        Pb[s, z, 0] = Pb[s, z, 0] + ZR[k, 0, 2] + ZR[k, 1, 1]
        Pb[s, z, 1] = Pb[s, z, 1] + ZR[k, 0, 1] + ZR[k, 1, 2]
        y_copy(k).start()

    def finish(k):
        s = k % SLOTS
        y_copy(k).wait_recv()
        OS[k] = Pb[s, z, yl] + YR[k]
        out_copy(k).start()

    def free(k):
        for kind in range(3):
            for d in range(2):
                z_copy(k, d, kind).wait_send()
        y_copy(k).wait_send()

    def step(k, carry):
        @pl.when(k < PH)
        def _():
            wait_rest(k)

            @pl.when(k >= SLOTS)
            def _():
                free(k - SLOTS)

            compute(k, k % SLOTS)
            send_first(k)

        @pl.when(k + 3 < PH)
        def _():
            own_y(k + 3).start()

        @pl.when(k + 2 < PH)
        def _():
            start_own_x(k + 2)

        @pl.when(k + 1 < PH)
        def _():
            start_fwd_x(k + 1)

        @pl.when(k + 2 < PH)
        def _():
            start_peer_x(k + 2)

        @pl.when((k >= 1) & (k < PH + 1))
        def _():
            relay(k - 1)

        @pl.when((k >= 2) & (k < PH + 2))
        def _():
            last(k - 2)

        @pl.when(k >= 3)
        def _():
            finish(k - 3)

        return carry

    lax.fori_loop(0, PH + 3, step, 0)

    def drain(k, carry):
        own_y(k).wait_send()
        for d in range(2):
            own_x(k, d).wait_send()
            peer_x(k, d).wait_send()
            fwd_x(k, d).wait_send()
        out_copy(k).wait()
        return carry

    lax.fori_loop(0, PH, drain, 0)
    lax.fori_loop(PH - SLOTS, PH, lambda k, carry: (free(k), carry)[1], 0)


def per_device(activations, out_grads, noise):
    dma = pltpu.SemaphoreType.DMA
    summed = pl.pallas_call(
        kernel,
        out_shape=jax.ShapeDtypeStruct((256, FL), F32),
        in_specs=[pl.BlockSpec(memory_space=pl.ANY)] * 2,
        out_specs=pl.BlockSpec(memory_space=pl.ANY),
        scratch_shapes=[
            pltpu.VMEM((2, TOK, FL), BF16),
            pltpu.VMEM((TOK, DL), BF16),
            pltpu.VMEM((2, PH, RW, TOK), BF16),
            pltpu.VMEM((PH, 8, 2, RW, TOK), BF16),
            pltpu.VMEM((8, 2 * GROWS, LANES), F32),
            pltpu.VMEM((8, 2 * GROWS, LANES), F32),
            pltpu.VMEM((8, LANES), F32),
            pltpu.VMEM((8, 8, LANES), F32),
            pltpu.VMEM((2, 8, 256), F32),
            pltpu.VMEM((SLOTS, 4, 2, RW, FL), F32),
            pltpu.VMEM((PH, 2, 3, RW, FL), F32),
            pltpu.VMEM((PH, RW, FL), F32),
            pltpu.VMEM((PH, RW, FL), F32),
            dma((EX,)),
            dma,
            dma((2,)),
            dma((2,)),
            dma,
            dma((8,)),
            dma((8,)),
            dma((8,)),
            dma((8,)),
            dma((2,)),
            dma((PH, 7)),
            dma((PH, 2, 3)),
            dma((PH,)),
            dma((SLOTS, 7)),
            dma((PH, 2, 3)),
            dma((PH,)),
            dma((PH,)),
        ],
        compiler_params=pltpu.CompilerParams(
            collective_id=0, has_side_effects=True, vmem_limit_bytes=62 << 20
        ),
        cost_estimate=pl.CostEstimate(flops=24 * 10**9, bytes_accessed=9 * 10**6, transcendentals=0),
    )(activations, out_grads)
    return (summed + noise) / COUNT


def solution(mesh):
    return jax.shard_map(
        per_device,
        mesh=mesh,
        in_specs=(P("dp", "tensor"), P("dp", "tensor"), P("dp", "tensor")),
        out_specs=P("dp", "tensor"),
        check_vma=False,
    )
```

time: 695 us -> 204 us (0.29)
  waiting for transfers between devices: 623 us -> 0 us
  Pallas kernels: 0 us -> 201 us
  matrix products: 54.1 us -> 0 us
  between operations: 13.1 us -> 0.02 us
    reduce_scatter x1 -> x0, waiting for transfers between devices: 308 us -> none  [per_device(): lax.psum_scatter(jnp.sum(each * factor[:, None, None], axis=0), 'dp', sca...]
    pallas_call x0 -> x1, Pallas kernels: none -> 201 us  [per_device(): pl.pallas_call(kernel, out_shape=jax.ShapeDtypeStruct((256, FL), F32), in...]
    all_gather x1 -> x0, waiting for transfers between devices: 165 us -> none  [per_device(): full_grads = lax.all_gather(out_grads, 'tensor', axis=1, tiled=True)]
    psum x1 -> x0, waiting for transfers between devices: 149 us -> none  [per_device(): act_gram, grad_gram = lax.psum((act_gram, grad_gram), 'tensor')]
    dot_general x3 -> x0, matrix products: 54.1 us -> none  [the longest x1 45.3 us: per_device(): jnp.einsum('bsd,bsf->bdf', columns, acts, preferred_element_type=jnp.floa...]
  transfers between devices with their start and end apart: 3 -> 0, of which waited for: 3 -> 0; matrix products, arithmetic and copies ran while one was open for 0% -> 0% of each run, Pallas kernels for 0% -> 0%
where the time goes in v1:
time: 204 us
  Pallas kernels  201 us (99%)
  other arithmetic  2.94 us (1%)
    pallas_call x1, Pallas kernels, per_device(): pl.pallas_call(kernel, out_shape=jax.ShapeDtypeStruct((256, FL), F32), in...  201 us

profile of v1, /device:TPU:0, one launch (start us, length us, event | category | flops | bytes accessed | tf_op | source)
XLA Modules:
  0.0 204.1 jit_solution(16152419018521773831)
XLA Ops:
  0.0 0.0 copy-start
  0.0 201.2 %shard_map.37 = f32[256,1792]{1,0:T(8,128)} custom-call(bf16[1536,1792]{1,0:T(8,128)(2,1)} %act.1, bf16[1536,512]{1,0:T(8,128)(2,1)} %g.1), custom_call_target="tpu_custom_call" | custom-call | flops 24000000000 | bytes 9000000 | tf_op jit(solution)/shard_map/pallas_call | solution.py:332
  201.2 0.0 copy-done
  201.2 2.9 %add_multiply_fusion = f32[256,1792]{1,0:T(8,128)} fusion(f32[256,1792]{1,0:T(8,128)} %shard_map.37, f32[256,1792]{1,0:T(8,128)S(1)} %copy-done), kind=kLoop, calls=%fused_computation | loop fusion | flops 917504 | bytes 5505024 | tf_op jit(solution)/shard_map/div | solution.py:374
Async XLA Ops:
  0.0 201.2 %copy-start = (f32[256,1792]{1,0:T(8,128)S(1)}, f32[256,1792]{1,0:T(8,128)}, u32[]{:S(2)}) copy-start(f32[256,1792]{1,0:T(8,128)} %param.5) | copy-start | bytes 5505028

commit v2 on v1

--- a/solution.py
+++ b/solution.py
@@ -20,6 +20,8 @@
 PH = 8
 RW = 32
 SLOTS = 4
+ZB = 5
+ZC = ZB * 256
 GROWS = EX * 32 + 8
 COUNT = 96
 LANES = 128
@@ -27,8 +29,8 @@
 
 def kernel(
     act, g, out,
-    H, gin, gT, Gb, GS, GR, SQm, SQ, FAC, Pb, ZR, YR, OS,
-    hsem, gsem, hx, gx, gl, gramS, gramR, sqS, sqR, facx, gsnd, grcv, gy, zsnd, zrcv, yrcv, osem,
+    H, gin, gT, Gb, GSA, GSG, RA1, A2, RA2, RG1, G2, RG2, SQm, SQ, FAC, Pz, Py, ZR, YR, YZ, WR, OS,
+    hsem, gsem, hx, gx, gl, gramS, gramR, sqS, sqR, facx, gsnd, grcv, gy, zsnd, zrcv, yrcv, wsnd, wrcv, y1rcv, osem,
 ):
     dp = lax.axis_index("dp")
     t = lax.axis_index("tensor")
@@ -64,7 +66,6 @@
     partners = [(dp, (t + j) % 8) for j in range(1, 8)] + [sib, up, down, ylo]
     for dev in partners:
         pl.semaphore_signal(barrier, inc=1, device_id=dev, device_id_type=MESH)
-    pl.semaphore_wait(barrier, len(partners))
 
     def shard_copy(k, owner, ssem, rsem, dev):
         return remote(Gb.at[k, owner], Gb.at[k, owner], ssem, rsem, dev)
@@ -106,7 +107,60 @@
         wait_shard(k, 0, 2)
         wait_shard(k, 1, 2)
 
+    i0 = lax.broadcasted_iota(jnp.int32, (LANES, LANES), 0)
+    i1 = lax.broadcasted_iota(jnp.int32, (LANES, LANES), 1)
+    e8 = lax.broadcasted_iota(jnp.int32, (8, LANES), 0)
+    nt = (((1,), (1,)), ((), ()))
+    zero8 = jnp.zeros((8, LANES), F32)
+
+    def gram(rows_of, piece):
+        def one(e, diags):
+            r = rows_of(e, pl.ds(pl.multiple_of(e * SEQ, SEQ), SEQ))
+            a = lax.dot_general(r, r, nt, preferred_element_type=F32)
+            packed = jnp.where(i0 >= i1, a[:LANES, :LANES], a[LANES:, LANES:])
+            below = a[LANES:, :LANES]
+            for owner in range(8):
+                part = packed if owner < 4 else below
+                lo = (owner % 4) * 32
+                piece(owner, pl.ds(pl.multiple_of(e * 32, 32), 32), part[lo : lo + 32])
+            diag = jnp.sum(jnp.where(i0 == i1, a[LANES:, LANES:], 0.0), axis=0, keepdims=True)
+            return jnp.where(e8 == e, diag, diags)
+
+        diags = lax.fori_loop(0, EX, one, zero8)
+        for owner in range(8):
+            piece(owner, slice(EX * 32, GROWS), diags)
+
+    def piece_a(owner, rows, value):
+        GSA[owner // 2, owner % 2, rows, :] = value
+
+    def piece_g(owner, rows, value):
+        GSG[owner % 2, owner // 2, rows, :] = value
+
+    def rows_h(e, rows):
+        h_in(e).wait()
+        return H[c, rows, :]
+
     g_in.wait()
+    gram(lambda e, rows: gin[rows, :], piece_g)
+    pl.semaphore_wait(barrier, len(partners))
+    g_one = remote(GSG.at[1 - yh], RG1, gramS.at[0], gramR.at[0], ypeer)
+    g_one.start()
+    gram(rows_h, piece_a)
+
+    def x_dev(j):
+        return (dp, ((x + j) % 4) * 2 + yh)
+
+    def a_one(j):
+        return remote(GSA.at[(x + j) % 4], RA1.at[x], gramS.at[j], gramR.at[j], x_dev(j))
+
+    def g_two(j):
+        return remote(G2.at[(x + j) % 4], RG2.at[x], gramS.at[3 + j], gramR.at[3 + j], x_dev(j))
+
+    for j in (2, 1, 3):
+        a_one(j).start()
+    h_sib = remote(H.at[c], H.at[c], hx.at[0], hx.at[1], sib)
+    h_sib.start()
+
     for e in range(EX):
         tr = gin[e * SEQ : (e + 1) * SEQ, :].T
         gT[:, :, :, e * SEQ : (e + 1) * SEQ] = tr.reshape(2, PH, RW, SEQ)
@@ -114,62 +168,29 @@
     g_sib = remote(gT.at[oc], Gb.at[:, t, c], gx.at[0], gx.at[1], sib)
     g_local.start()
     g_sib.start()
-    for e in range(EX):
-        h_in(e).wait()
-    h_sib = remote(H.at[c], H.at[c], hx.at[0], hx.at[1], sib)
-    h_sib.start()
+
+    g_one.wait_recv()
+    G2[...] = GSG[yh] + RG1[...]
+    for j in (2, 1, 3):
+        g_two(j).start()
     g_local.wait()
     g_sib.wait()
     for k in range(2):
         own_y(k).start()
+    for j in range(1, 4):
+        a_one(j).wait_recv()
+    RA1[x] = GSA[x]
+    A2[...] = (RA1[0] + RA1[1]) + (RA1[2] + RA1[3])
+    a_two = remote(A2.at[1 - yh], RA2, gramS.at[7], gramR.at[7], ypeer)
+    a_two.start()
     start_own_x(0)
-
-    i0 = lax.broadcasted_iota(jnp.int32, (LANES, LANES), 0)
-    i1 = lax.broadcasted_iota(jnp.int32, (LANES, LANES), 1)
-    e8 = lax.broadcasted_iota(jnp.int32, (8, LANES), 0)
-    nt = (((1,), (1,)), ((), ()))
-
-    def gram(e, diags):
-        rows = pl.ds(pl.multiple_of(e * SEQ, SEQ), SEQ)
-        result = []
-        for m in range(2):
-            r = H[c, rows, :] if m == 0 else gin[rows, :]
-            a = lax.dot_general(r, r, nt, preferred_element_type=F32)
-            packed = jnp.where(i0 >= i1, a[:LANES, :LANES], a[LANES:, LANES:])
-            below = a[LANES:, :LANES]
-            for r8 in range(8):
-                part = packed if r8 < 4 else below
-                lo = (r8 % 4) * 32
-                GS[r8, pl.ds(pl.multiple_of(m * GROWS + e * 32, 8), 32), :] = part[lo : lo + 32]
-            diag = jnp.sum(jnp.where(i0 == i1, a[LANES:, LANES:], 0.0), axis=0, keepdims=True)
-            result.append(jnp.where(e8 == e, diag, diags[m]))
-        return tuple(result)
-
-    zero8 = jnp.zeros((8, LANES), F32)
-    diags = lax.fori_loop(0, EX, gram, (zero8, zero8))
-    for m in range(2):
-        for r8 in range(8):
-            GS[r8, m * GROWS + EX * 32 : (m + 1) * GROWS, :] = diags[m]
-
-    def gram_copy(j):
-        peer = (t + j) % 8
-        return remote(GS.at[peer], GR.at[t], gramS.at[j], gramR.at[j], (dp, peer))
-
-    for j in range(1, 8):
-        gram_copy(j).start()
-    GR[t] = GS[t]
-    start_peer_x(0)
-    own_y(2).start()
-    start_own_x(1)
-    start_fwd_x(0)
-    start_peer_x(1)
-    for j in range(1, 8):
-        gram_copy(j).wait_recv()
-
-    total = GR[0]
-    for s in range(1, 8):
-        total = total + GR[s]
-    prod = total[:GROWS] * total[GROWS:]
+    for j in range(1, 4):
+        g_two(j).wait_recv()
+    RG2[x] = G2[x]
+    grad_gram = (RG2[0] + RG2[1]) + (RG2[2] + RG2[3])
+    a_two.wait_recv()
+    prod = (A2[yh] + RA2[...]) * grad_gram
+
     r32 = lax.broadcasted_iota(jnp.int32, (32, LANES), 0)
     l32 = lax.broadcasted_iota(jnp.int32, (32, LANES), 1)
     weight = jnp.where(l32 == r32 + t * 32, 1.0, 2.0)
@@ -187,6 +208,9 @@
 
     for j in range(1, 8):
         sq_copy(j).start()
+    start_peer_x(0)
+    own_y(2).start()
+    start_own_x(1)
     for j in range(1, 8):
         sq_copy(j).wait_recv()
     sq = SQ[0]
@@ -198,14 +222,20 @@
     FAC[c] = jnp.broadcast_to(factor, (8, 256))
     fac_sib = remote(FAC.at[c], FAC.at[c], facx.at[0], facx.at[1], sib)
     fac_sib.start()
+    start_fwd_x(0)
+    start_peer_x(1)
     h_sib.wait()
     fac_sib.wait()
+    g_one.wait_send()
+    a_two.wait_send()
+    for j in range(1, 4):
+        a_one(j).wait_send()
+        g_two(j).wait_send()
     for j in range(1, 8):
-        gram_copy(j).wait_send()
         sq_copy(j).wait_send()
 
     def compute(k, s):
-        def block(n, carry):
+        def block(n):
             cols = pl.ds(pl.multiple_of(n * 256, 256), 256)
             acc = None
             for e in range(2 * EX):
@@ -214,61 +244,108 @@
                 rhs = H[cs, j * SEQ : (j + 1) * SEQ, cols]
                 d = jnp.dot(lhs, rhs, preferred_element_type=F32) * FAC[cs, j : j + 1, :]
                 acc = d if acc is None else acc + d
-            Pb[s, :, :, :, cols] = acc.reshape(4, 2, RW, 256)
+            return acc.reshape(4, 2, RW, 256)
+
+        def to_z(n, carry):
+            Pz[s, :, :, :, pl.ds(pl.multiple_of(n * 256, 256), 256)] = block(n)
             return carry
 
-        lax.fori_loop(0, FL // 256, block, 0)
+        def to_y(n, carry):
+            r = block(n + ZB)
+            for b in range(2):
+                Py[s, b, :, n] = r[:, b]
+            return carry
+
+        lax.fori_loop(0, 2, to_y, 0)
+        y1_copy(k).start()
+        lax.fori_loop(0, ZB, to_z, 0)
+
+    def pick(d, kind):
+        if kind == 0:
+            return zo, d
+        if kind == 1:
+            return (zp, 1) if d == 0 else (zm, 0)
+        return (zp, 0) if d == 0 else (zm, 1)
 
     def z_copy(k, d, kind):
         s = k % SLOTS
-        if kind == 0:
-            src = Pb.at[s, zo, d]
-        elif kind == 1:
-            src = Pb.at[s, zp, 1] if d == 0 else Pb.at[s, zm, 0]
-        else:
-            src = Pb.at[s, zp, 0] if d == 0 else Pb.at[s, zm, 1]
-        return remote(src, ZR.at[k, d, kind], zsnd.at[s, 2 * kind + d], zrcv.at[k, d, kind], up if d == 0 else down)
+        a, b = pick(d, kind)
+        return remote(
+            Pz.at[s, a, b], ZR.at[k, d, kind], zsnd.at[s, 2 * kind + d], zrcv.at[k, d, kind], up if d == 0 else down
+        )
 
     def y_copy(k):
         s = k % SLOTS
-        return remote(Pb.at[s, z, 1 - yl], YR.at[k], zsnd.at[s, 6], yrcv.at[k], ylo)
+        return remote(Pz.at[s, z, 1 - yl], YR.at[k], zsnd.at[s, 6], yrcv.at[k], ylo)
+
+    def y1_copy(k):
+        s = k % SLOTS
+        return remote(Py.at[s, 1 - yl], YZ.at[k], wsnd.at[s, 6], y1rcv.at[k], ylo)
+
+    def w_copy(k, d, kind):
+        s = k % SLOTS
+        a, b = pick(d, kind)
+        return remote(
+            Py.at[s, yl, a, b], WR.at[k, d, kind], wsnd.at[s, 2 * kind + d], wrcv.at[k, d, kind], up if d == 0 else down
+        )
 
     def out_copy(k):
         return pltpu.make_async_copy(OS.at[k], out.at[pl.ds(pl.multiple_of(k * RW, RW), RW)], osem.at[k])
 
-    def send_first(k):
+    def send_first(copy, k):
         for kind in range(2):
             for d in range(2):
-                z_copy(k, d, kind).start()
-
-    def relay(k):
+                copy(k, d, kind).start()
+
+    def z_relay(k):
         s = k % SLOTS
         for d in range(2):
             z_copy(k, d, 0).wait_recv()
-            dest = (zp, 0) if d == 0 else (zm, 1)
-            Pb[s, dest[0], dest[1]] = Pb[s, dest[0], dest[1]] + ZR[k, d, 0]
+            a, b = pick(d, 2)
+            Pz[s, a, b] = Pz[s, a, b] + ZR[k, d, 0]
             z_copy(k, d, 2).start()
 
-    def last(k):
+    def w_first(k):
+        s = k % SLOTS
+        y1_copy(k).wait_recv()
+        Py[s, yl] = Py[s, yl] + YZ[k]
+        send_first(w_copy, k)
+
+    def w_relay(k):
+        s = k % SLOTS
+        for d in range(2):
+            w_copy(k, d, 0).wait_recv()
+            a, b = pick(d, 2)
+            Py[s, yl, a, b] = Py[s, yl, a, b] + WR[k, d, 0]
+            w_copy(k, d, 2).start()
+
+    def z_last(k):
         s = k % SLOTS
         for kind in (1, 2):
             for d in range(2):
                 z_copy(k, d, kind).wait_recv()
-        Pb[s, z, 0] = Pb[s, z, 0] + ZR[k, 0, 2] + ZR[k, 1, 1]
-        Pb[s, z, 1] = Pb[s, z, 1] + ZR[k, 0, 1] + ZR[k, 1, 2]
+        Pz[s, z, 0] = Pz[s, z, 0] + ZR[k, 0, 2] + ZR[k, 1, 1]
+        Pz[s, z, 1] = Pz[s, z, 1] + ZR[k, 0, 1] + ZR[k, 1, 2]
         y_copy(k).start()
 
     def finish(k):
         s = k % SLOTS
+        for kind in (1, 2):
+            for d in range(2):
+                w_copy(k, d, kind).wait_recv()
+        OS[k, :, ZC : ZC + 256] = Py[s, yl, z, 0] + WR[k, 0, 2] + WR[k, 1, 1]
+        OS[k, :, ZC + 256 :] = Py[s, yl, z, 1] + WR[k, 0, 1] + WR[k, 1, 2]
         y_copy(k).wait_recv()
-        OS[k] = Pb[s, z, yl] + YR[k]
+        OS[k, :, :ZC] = Pz[s, z, yl] + YR[k]
         out_copy(k).start()
 
     def free(k):
         for kind in range(3):
             for d in range(2):
                 z_copy(k, d, kind).wait_send()
+                w_copy(k, d, kind).wait_send()
         y_copy(k).wait_send()
+        y1_copy(k).wait_send()
 
     def step(k, carry):
         @pl.when(k < PH)
@@ -280,7 +357,11 @@
                 free(k - SLOTS)
 
             compute(k, k % SLOTS)
-            send_first(k)
+            send_first(z_copy, k)
+
+        @pl.when((k >= 1) & (k < PH + 1))
+        def _():
+            z_relay(k - 1)
 
         @pl.when(k + 3 < PH)
         def _():
@@ -300,11 +381,12 @@
 
         @pl.when((k >= 1) & (k < PH + 1))
         def _():
-            relay(k - 1)
+            w_first(k - 1)
 
         @pl.when((k >= 2) & (k < PH + 2))
         def _():
-            last(k - 2)
+            z_last(k - 2)
+            w_relay(k - 2)
 
         @pl.when(k >= 3)
         def _():
@@ -339,14 +421,23 @@
             pltpu.VMEM((TOK, DL), BF16),
             pltpu.VMEM((2, PH, RW, TOK), BF16),
             pltpu.VMEM((PH, 8, 2, RW, TOK), BF16),
-            pltpu.VMEM((8, 2 * GROWS, LANES), F32),
-            pltpu.VMEM((8, 2 * GROWS, LANES), F32),
+            pltpu.VMEM((4, 2, GROWS, LANES), F32),
+            pltpu.VMEM((2, 4, GROWS, LANES), F32),
+            pltpu.VMEM((4, 2, GROWS, LANES), F32),
+            pltpu.VMEM((2, GROWS, LANES), F32),
+            pltpu.VMEM((GROWS, LANES), F32),
+            pltpu.VMEM((4, GROWS, LANES), F32),
+            pltpu.VMEM((4, GROWS, LANES), F32),
+            pltpu.VMEM((4, GROWS, LANES), F32),
             pltpu.VMEM((8, LANES), F32),
             pltpu.VMEM((8, 8, LANES), F32),
             pltpu.VMEM((2, 8, 256), F32),
-            pltpu.VMEM((SLOTS, 4, 2, RW, FL), F32),
-            pltpu.VMEM((PH, 2, 3, RW, FL), F32),
-            pltpu.VMEM((PH, RW, FL), F32),
+            pltpu.VMEM((SLOTS, 4, 2, RW, ZC), F32),
+            pltpu.VMEM((SLOTS, 2, 4, 2, RW, 256), F32),
+            pltpu.VMEM((PH, 2, 3, RW, ZC), F32),
+            pltpu.VMEM((PH, RW, ZC), F32),
+            pltpu.VMEM((PH, 4, 2, RW, 256), F32),
+            pltpu.VMEM((PH, 2, 3, RW, 256), F32),
             pltpu.VMEM((PH, RW, FL), F32),
             dma((EX,)),
             dma,
@@ -364,6 +455,9 @@
             dma((SLOTS, 7)),
             dma((PH, 2, 3)),
             dma((PH,)),
+            dma((SLOTS, 7)),
+            dma((PH, 2, 3)),
+            dma((PH,)),
             dma((PH,)),
         ],
         compiler_params=pltpu.CompilerParams(

time: 204 us -> 173 us (0.85)
  Pallas kernels: 201 us -> 170 us
    pallas_call x1, Pallas kernels: 201 us -> 170 us  [per_device(): pl.pallas_call(kernel, out_shape=jax.ShapeDtypeStruct((256, FL), F32), in...]
where the time goes in v2:
time: 173 us
  Pallas kernels  170 us (98%)
  other arithmetic  2.94 us (2%)
    pallas_call x1, Pallas kernels, per_device(): pl.pallas_call(kernel, out_shape=jax.ShapeDtypeStruct((256, FL), F32), in...  170 us

profile of v2, /device:TPU:0, one launch (start us, length us, event | category | flops | bytes accessed | tf_op | source)
XLA Modules:
  0.0 173.0 jit_solution(906595996300520738)
XLA Ops:
  0.0 0.0 copy-start
  0.0 170.0 %shard_map.37 = f32[256,1792]{1,0:T(8,128)} custom-call(bf16[1536,1792]{1,0:T(8,128)(2,1)} %act.1, bf16[1536,512]{1,0:T(8,128)(2,1)} %g.1), custom_call_target="tpu_custom_call" | custom-call | flops 24000000000 | bytes 9000000 | tf_op jit(solution)/shard_map/pallas_call | solution.py:414
  170.1 0.0 copy-done
  170.1 2.9 %add_multiply_fusion = f32[256,1792]{1,0:T(8,128)} fusion(f32[256,1792]{1,0:T(8,128)} %shard_map.37, f32[256,1792]{1,0:T(8,128)S(1)} %copy-done), kind=kLoop, calls=%fused_computation | loop fusion | flops 917504 | bytes 5505024 | tf_op jit(solution)/shard_map/div | solution.py:468
Async XLA Ops:
  0.0 170.1 %copy-start = (f32[256,1792]{1,0:T(8,128)S(1)}, f32[256,1792]{1,0:T(8,128)}, u32[]{:S(2)}) copy-start(f32[256,1792]{1,0:T(8,128)} %param.5) | copy-start | bytes 5505028

commit v3 on v2

--- a/solution.py
+++ b/solution.py
@@ -17,20 +17,26 @@
 TOK = EX * SEQ
 FL = 1792
 DL = 512
-PH = 8
-RW = 32
+PH = 16
+RW = 16
+GP = 9
 SLOTS = 4
 ZB = 5
 ZC = ZB * 256
+MC = ZC + 256
 GROWS = EX * 32 + 8
 COUNT = 96
 LANES = 128
 
 
+class Single(int):
+    pass
+
+
 def kernel(
     act, g, out,
-    H, gin, gT, Gb, GSA, GSG, RA1, A2, RA2, RG1, G2, RG2, SQm, SQ, FAC, Pz, Py, ZR, YR, YZ, WR, OS,
-    hsem, gsem, hx, gx, gl, gramS, gramR, sqS, sqR, facx, gsnd, grcv, gy, zsnd, zrcv, yrcv, wsnd, wrcv, y1rcv, osem,
+    H, gin, gT, Gb, GSA, GSG, RA1, A2, RA2, RG1, G2, RG2, SQm, SQ, FAC, Pz, Py, ZR, YR, YZ, OS,
+    hsem, gsem, hx, gx, gl, gramS, gramR, sqS, sqR, facx, gsnd, grcv, gy, zsnd, zrcv, yrcv, y1rcv, osem,
 ):
     dp = lax.axis_index("dp")
     t = lax.axis_index("tensor")
@@ -68,7 +74,11 @@
         pl.semaphore_signal(barrier, inc=1, device_id=dev, device_id_type=MESH)
 
     def shard_copy(k, owner, ssem, rsem, dev):
-        return remote(Gb.at[k, owner], Gb.at[k, owner], ssem, rsem, dev)
+        if isinstance(k, Single):
+            part = Gb.at[pl.ds(2 * k - k // 8, 1), owner]
+        else:
+            part = Gb.at[pl.ds(2 * k - 1, 2), owner]
+        return remote(part, part, ssem, rsem, dev)
 
     def own_y(k):
         return shard_copy(k, t, gsnd.at[k, 0], gy.at[k], ypeer)
@@ -141,10 +151,21 @@
         return H[c, rows, :]
 
     g_in.wait()
+    for e in range(EX):
+        tr = gin[e * SEQ : (e + 1) * SEQ, :].T
+        gT[:, :, :, e * SEQ : (e + 1) * SEQ] = tr.reshape(2, PH, RW, SEQ)
+    g_local = pltpu.make_async_copy(gT.at[c], Gb.at[:, t, c], gl)
+    g_local.start()
+    pl.semaphore_wait(barrier, len(partners))
+    g_sib = remote(gT.at[oc], Gb.at[:, t, c], gx.at[0], gx.at[1], sib)
+    g_sib.start()
     gram(lambda e, rows: gin[rows, :], piece_g)
-    pl.semaphore_wait(barrier, len(partners))
     g_one = remote(GSG.at[1 - yh], RG1, gramS.at[0], gramR.at[0], ypeer)
     g_one.start()
+    g_local.wait()
+    g_sib.wait()
+    own_y(Single(0)).start()
+    start_own_x(Single(0))
     gram(rows_h, piece_a)
 
     def x_dev(j):
@@ -161,29 +182,18 @@
     h_sib = remote(H.at[c], H.at[c], hx.at[0], hx.at[1], sib)
     h_sib.start()
 
-    for e in range(EX):
-        tr = gin[e * SEQ : (e + 1) * SEQ, :].T
-        gT[:, :, :, e * SEQ : (e + 1) * SEQ] = tr.reshape(2, PH, RW, SEQ)
-    g_local = pltpu.make_async_copy(gT.at[c], Gb.at[:, t, c], gl)
-    g_sib = remote(gT.at[oc], Gb.at[:, t, c], gx.at[0], gx.at[1], sib)
-    g_local.start()
-    g_sib.start()
-
     g_one.wait_recv()
     G2[...] = GSG[yh] + RG1[...]
     for j in (2, 1, 3):
         g_two(j).start()
-    g_local.wait()
-    g_sib.wait()
-    for k in range(2):
-        own_y(k).start()
+    start_peer_x(Single(0))
     for j in range(1, 4):
         a_one(j).wait_recv()
     RA1[x] = GSA[x]
     A2[...] = (RA1[0] + RA1[1]) + (RA1[2] + RA1[3])
     a_two = remote(A2.at[1 - yh], RA2, gramS.at[7], gramR.at[7], ypeer)
     a_two.start()
-    start_own_x(0)
+    start_own_x(1)
     for j in range(1, 4):
         g_two(j).wait_recv()
     RG2[x] = G2[x]
@@ -208,9 +218,9 @@
 
     for j in range(1, 8):
         sq_copy(j).start()
-    start_peer_x(0)
-    own_y(2).start()
-    start_own_x(1)
+    start_fwd_x(Single(0))
+    for k in range(1, 4):
+        own_y(k).start()
     for j in range(1, 8):
         sq_copy(j).wait_recv()
     sq = SQ[0]
@@ -222,8 +232,8 @@
     FAC[c] = jnp.broadcast_to(factor, (8, 256))
     fac_sib = remote(FAC.at[c], FAC.at[c], facx.at[0], facx.at[1], sib)
     fac_sib.start()
-    start_fwd_x(0)
     start_peer_x(1)
+    start_own_x(2)
     h_sib.wait()
     fac_sib.wait()
     g_one.wait_send()
@@ -234,31 +244,32 @@
     for j in range(1, 8):
         sq_copy(j).wait_send()
 
-    def compute(k, s):
-        def block(n):
-            cols = pl.ds(pl.multiple_of(n * 256, 256), 256)
-            acc = None
-            for e in range(2 * EX):
-                cs, j = divmod(e, EX)
-                lhs = Gb[k, :, cs, :, j * SEQ : (j + 1) * SEQ].reshape(8 * RW, SEQ)
-                rhs = H[cs, j * SEQ : (j + 1) * SEQ, cols]
-                d = jnp.dot(lhs, rhs, preferred_element_type=F32) * FAC[cs, j : j + 1, :]
-                acc = d if acc is None else acc + d
-            return acc.reshape(4, 2, RW, 256)
-
-        def to_z(n, carry):
-            Pz[s, :, :, :, pl.ds(pl.multiple_of(n * 256, 256), 256)] = block(n)
+    def block(k, n):
+        cols = pl.ds(pl.multiple_of(n * 256, 256), 256)
+        acc = None
+        for e in range(2 * EX):
+            cs, j = divmod(e, EX)
+            lhs = Gb[k, :, cs, :, j * SEQ : (j + 1) * SEQ].reshape(8 * RW, SEQ)
+            rhs = H[cs, j * SEQ : (j + 1) * SEQ, cols]
+            d = jnp.dot(lhs, rhs, preferred_element_type=F32) * FAC[cs, j : j + 1, :]
+            acc = d if acc is None else acc + d
+        return acc.reshape(4, 2, RW, 256)
+
+    def compute_y(k):
+        def one(n, carry):
+            r = block(k, n + ZB)
+            for b in range(2):
+                Py[k % SLOTS, b, :, n] = r[:, b]
             return carry
 
-        def to_y(n, carry):
-            r = block(n + ZB)
-            for b in range(2):
-                Py[s, b, :, n] = r[:, b]
+        lax.fori_loop(0, 2, one, 0)
+
+    def compute_z(k):
+        def one(n, carry):
+            Pz[k % SLOTS, :, :, :, pl.ds(pl.multiple_of(n * 256, 256), 256)] = block(k, n)
             return carry
 
-        lax.fori_loop(0, 2, to_y, 0)
-        y1_copy(k).start()
-        lax.fori_loop(0, ZB, to_z, 0)
+        lax.fori_loop(0, ZB, one, 0)
 
     def pick(d, kind):
         if kind == 0:
@@ -267,126 +278,156 @@
             return (zp, 1) if d == 0 else (zm, 0)
         return (zp, 0) if d == 0 else (zm, 1)
 
-    def z_copy(k, d, kind):
+    def z_copy(k, d, kind, cols=slice(0, MC)):
         s = k % SLOTS
         a, b = pick(d, kind)
         return remote(
-            Pz.at[s, a, b], ZR.at[k, d, kind], zsnd.at[s, 2 * kind + d], zrcv.at[k, d, kind], up if d == 0 else down
+            Pz.at[s, a, b, :, cols],
+            ZR.at[k, d, kind, :, cols],
+            zsnd.at[s, 2 * kind + d],
+            zrcv.at[k, d, kind],
+            up if d == 0 else down,
         )
+
+    late = slice(ZC, MC)
 
     def y_copy(k):
         s = k % SLOTS
-        return remote(Pz.at[s, z, 1 - yl], YR.at[k], zsnd.at[s, 6], yrcv.at[k], ylo)
+        return remote(Pz.at[s, z, 1 - yl, :, 0:ZC], YR.at[k], zsnd.at[s, 6], yrcv.at[k], ylo)
 
     def y1_copy(k):
         s = k % SLOTS
-        return remote(Py.at[s, 1 - yl], YZ.at[k], wsnd.at[s, 6], y1rcv.at[k], ylo)
-
-    def w_copy(k, d, kind):
-        s = k % SLOTS
-        a, b = pick(d, kind)
-        return remote(
-            Py.at[s, yl, a, b], WR.at[k, d, kind], wsnd.at[s, 2 * kind + d], wrcv.at[k, d, kind], up if d == 0 else down
-        )
+        return remote(Py.at[s, 1 - yl], YZ.at[k], zsnd.at[s, 7], y1rcv.at[k], ylo)
 
     def out_copy(k):
         return pltpu.make_async_copy(OS.at[k], out.at[pl.ds(pl.multiple_of(k * RW, RW), RW)], osem.at[k])
 
-    def send_first(copy, k):
+    def add_y1(k):
+        y1_copy(k).wait_recv()
+        Pz[(k + 1) % SLOTS, :, :, :, late] = Py[k % SLOTS, yl] + YZ[k]
+
+    def z_first(k, cols):
         for kind in range(2):
             for d in range(2):
-                copy(k, d, kind).start()
-
-    def z_relay(k):
+                z_copy(k, d, kind, cols).start()
+
+    def z_relay(k, cols):
         s = k % SLOTS
         for d in range(2):
-            z_copy(k, d, 0).wait_recv()
+            z_copy(k, d, 0, cols).wait_recv()
             a, b = pick(d, 2)
-            Pz[s, a, b] = Pz[s, a, b] + ZR[k, d, 0]
-            z_copy(k, d, 2).start()
-
-    def w_first(k):
-        s = k % SLOTS
-        y1_copy(k).wait_recv()
-        Py[s, yl] = Py[s, yl] + YZ[k]
-        send_first(w_copy, k)
-
-    def w_relay(k):
-        s = k % SLOTS
-        for d in range(2):
-            w_copy(k, d, 0).wait_recv()
-            a, b = pick(d, 2)
-            Py[s, yl, a, b] = Py[s, yl, a, b] + WR[k, d, 0]
-            w_copy(k, d, 2).start()
-
-    def z_last(k):
-        s = k % SLOTS
+            Pz[s, a, b, :, cols] = Pz[s, a, b, :, cols] + ZR[k, d, 0, :, cols]
+            z_copy(k, d, 2, cols).start()
+
+    def z_wait(k, cols):
         for kind in (1, 2):
             for d in range(2):
-                z_copy(k, d, kind).wait_recv()
-        Pz[s, z, 0] = Pz[s, z, 0] + ZR[k, 0, 2] + ZR[k, 1, 1]
-        Pz[s, z, 1] = Pz[s, z, 1] + ZR[k, 0, 1] + ZR[k, 1, 2]
+                z_copy(k, d, kind, cols).wait_recv()
+
+    def z_sum(k, b, cols):
+        one, two = (2, 1) if b == 0 else (1, 2)
+        return Pz[k % SLOTS, z, b, :, cols] + ZR[k, 0, one, :, cols] + ZR[k, 1, two, :, cols]
+
+    def store_late(k):
+        for b in range(2):
+            OS[k - 1, :, ZC + 256 * b : ZC + 256 * (b + 1)] = z_sum(k, b, late)
+
+    def z_last(k):
+        z_wait(k, slice(0, MC))
+        for b in range(2):
+            Pz[k % SLOTS, z, b, :, 0:ZC] = z_sum(k, b, slice(0, ZC))
         y_copy(k).start()
+
+        @pl.when(k >= 1)
+        def _():
+            store_late(k)
 
     def finish(k):
         s = k % SLOTS
-        for kind in (1, 2):
-            for d in range(2):
-                w_copy(k, d, kind).wait_recv()
-        OS[k, :, ZC : ZC + 256] = Py[s, yl, z, 0] + WR[k, 0, 2] + WR[k, 1, 1]
-        OS[k, :, ZC + 256 :] = Py[s, yl, z, 1] + WR[k, 0, 1] + WR[k, 1, 2]
         y_copy(k).wait_recv()
-        OS[k, :, :ZC] = Pz[s, z, yl] + YR[k]
+        OS[k, :, 0:ZC] = Pz[s, z, yl, :, 0:ZC] + YR[k]
         out_copy(k).start()
 
     def free(k):
         for kind in range(3):
             for d in range(2):
                 z_copy(k, d, kind).wait_send()
-                w_copy(k, d, kind).wait_send()
         y_copy(k).wait_send()
         y1_copy(k).wait_send()
 
+    Pz[0, :, :, :, late] = jnp.zeros((4, 2, RW, MC - ZC), F32)
+
     def step(k, carry):
+        j = k // 2
+        even = k % 2 == 0
+
+        @pl.when((~even) & (k < PH - 1))
+        def _():
+            wait_rest(j + 1)
+
+        for p, now in ((0, 0), (8, PH - 1)):
+
+            @pl.when(k == now)
+            def _():
+                wait_rest(Single(p))
+
+        @pl.when((k >= SLOTS) & (k <= PH))
+        def _():
+            free(k - SLOTS)
+
         @pl.when(k < PH)
         def _():
-            wait_rest(k)
-
-            @pl.when(k >= SLOTS)
+            compute_y(k)
+            y1_copy(k).start()
+            compute_z(k)
+
+        @pl.when((k >= 1) & (k <= PH))
+        def _():
+            add_y1(k - 1)
+
+        @pl.when(k < PH)
+        def _():
+            z_first(k, slice(0, MC))
+
+        @pl.when(k == PH)
+        def _():
+            z_first(k, late)
+
+        @pl.when((k >= 1) & (k <= PH))
+        def _():
+            z_relay(k - 1, slice(0, MC))
+
+        @pl.when(k == PH + 1)
+        def _():
+            z_relay(PH, late)
+
+        @pl.when(k == 0)
+        def _():
+            start_fwd_x(1)
+            start_peer_x(2)
+
+        def at(when, op, ahead, last):
+            @pl.when(when & (j + ahead < GP - 1))
             def _():
-                free(k - SLOTS)
-
-            compute(k, k % SLOTS)
-            send_first(z_copy, k)
-
-        @pl.when((k >= 1) & (k < PH + 1))
-        def _():
-            z_relay(k - 1)
-
-        @pl.when(k + 3 < PH)
-        def _():
-            own_y(k + 3).start()
-
-        @pl.when(k + 2 < PH)
-        def _():
-            start_own_x(k + 2)
-
-        @pl.when(k + 1 < PH)
-        def _():
-            start_fwd_x(k + 1)
-
-        @pl.when(k + 2 < PH)
-        def _():
-            start_peer_x(k + 2)
-
-        @pl.when((k >= 1) & (k < PH + 1))
-        def _():
-            w_first(k - 1)
-
-        @pl.when((k >= 2) & (k < PH + 2))
+                op(j + ahead)
+
+            @pl.when(k == last)
+            def _():
+                op(Single(GP - 1))
+
+        at(~even, start_fwd_x, 2, 13)
+        at(~even, start_peer_x, 3, 11)
+        at(even, start_own_x, 3, 10)
+        at(even, lambda p: own_y(p).start(), 4, 8)
+
+        @pl.when((k >= 2) & (k <= PH + 1))
         def _():
             z_last(k - 2)
-            w_relay(k - 2)
+
+        @pl.when(k == PH + 2)
+        def _():
+            z_wait(PH, late)
+            store_late(PH)
 
         @pl.when(k >= 3)
         def _():
@@ -402,11 +443,16 @@
             own_x(k, d).wait_send()
             peer_x(k, d).wait_send()
             fwd_x(k, d).wait_send()
-        out_copy(k).wait()
         return carry
 
-    lax.fori_loop(0, PH, drain, 0)
-    lax.fori_loop(PH - SLOTS, PH, lambda k, carry: (free(k), carry)[1], 0)
+    lax.fori_loop(1, GP - 1, drain, 0)
+    drain(Single(0), 0)
+    drain(Single(GP - 1), 0)
+    lax.fori_loop(PH - SLOTS + 1, PH, lambda k, carry: (free(k), carry)[1], 0)
+    for kind in range(3):
+        for d in range(2):
+            z_copy(PH, d, kind, late).wait_send()
+    lax.fori_loop(0, PH, lambda k, carry: (out_copy(k).wait(), carry)[1], 0)
 
 
 def per_device(activations, out_grads, noise):
@@ -432,12 +478,11 @@
             pltpu.VMEM((8, LANES), F32),
             pltpu.VMEM((8, 8, LANES), F32),
             pltpu.VMEM((2, 8, 256), F32),
-            pltpu.VMEM((SLOTS, 4, 2, RW, ZC), F32),
+            pltpu.VMEM((SLOTS, 4, 2, RW, MC), F32),
             pltpu.VMEM((SLOTS, 2, 4, 2, RW, 256), F32),
-            pltpu.VMEM((PH, 2, 3, RW, ZC), F32),
+            pltpu.VMEM((PH + 1, 2, 3, RW, MC), F32),
             pltpu.VMEM((PH, RW, ZC), F32),
             pltpu.VMEM((PH, 4, 2, RW, 256), F32),
-            pltpu.VMEM((PH, 2, 3, RW, 256), F32),
             pltpu.VMEM((PH, RW, FL), F32),
             dma((EX,)),
             dma,
@@ -449,14 +494,12 @@
             dma((8,)),
             dma((8,)),
             dma((2,)),
-            dma((PH, 7)),
-            dma((PH, 2, 3)),
+            dma((GP, 7)),
+            dma((GP, 2, 3)),
+            dma((GP,)),
+            dma((SLOTS, 8)),
+            dma((PH + 1, 2, 3)),
             dma((PH,)),
-            dma((SLOTS, 7)),
-            dma((PH, 2, 3)),
-            dma((PH,)),
-            dma((SLOTS, 7)),
-            dma((PH, 2, 3)),
             dma((PH,)),
             dma((PH,)),
         ],

time: 173 us -> 164 us (0.948)
  Pallas kernels: 170 us -> 160 us
    pallas_call x1, Pallas kernels: 170 us -> 160 us  [per_device(): pl.pallas_call(kernel, out_shape=jax.ShapeDtypeStruct((256, FL), F32), in...]
where the time goes in v3:
time: 164 us; the launch traced here: 163 us
  Pallas kernels  160 us (98%)
  other arithmetic  2.94 us (2%)
    pallas_call x1, Pallas kernels, per_device(): pl.pallas_call(kernel, out_shape=jax.ShapeDtypeStruct((256, FL), F32), in...  160 us

profile of v3, /device:TPU:0, one launch (start us, length us, event | category | flops | bytes accessed | tf_op | source)
XLA Modules:
  0.0 163.3 jit_solution(13342679576493633751)
XLA Ops:
  0.0 0.0 copy-start
  0.0 160.3 %shard_map.37 = f32[256,1792]{1,0:T(8,128)} custom-call(bf16[1536,1792]{1,0:T(8,128)(2,1)} %act.1, bf16[1536,512]{1,0:T(8,128)(2,1)} %g.1), custom_call_target="tpu_custom_call" | custom-call | flops 24000000000 | bytes 9000000 | tf_op jit(solution)/shard_map/pallas_call | solution.py:460
  160.4 0.0 copy-done
  160.4 2.9 %add_multiply_fusion = f32[256,1792]{1,0:T(8,128)} fusion(f32[256,1792]{1,0:T(8,128)} %shard_map.37, f32[256,1792]{1,0:T(8,128)S(1)} %copy-done), kind=kLoop, calls=%fused_computation | loop fusion | flops 917504 | bytes 5505024 | tf_op jit(solution)/shard_map/div | solution.py:511
Async XLA Ops:
  0.0 160.4 %copy-start = (f32[256,1792]{1,0:T(8,128)S(1)}, f32[256,1792]{1,0:T(8,128)}, u32[]{:S(2)}) copy-start(f32[256,1792]{1,0:T(8,128)} %param.5) | copy-start | bytes 5505028

commit v4 on v3

--- a/solution.py
+++ b/solution.py
@@ -19,7 +19,6 @@
 DL = 512
 PH = 16
 RW = 16
-GP = 9
 SLOTS = 4
 ZB = 5
 ZC = ZB * 256
@@ -27,10 +26,6 @@
 GROWS = EX * 32 + 8
 COUNT = 96
 LANES = 128
-
-
-class Single(int):
-    pass
 
 
 def kernel(
@@ -74,10 +69,7 @@
         pl.semaphore_signal(barrier, inc=1, device_id=dev, device_id_type=MESH)
 
     def shard_copy(k, owner, ssem, rsem, dev):
-        if isinstance(k, Single):
-            part = Gb.at[pl.ds(2 * k - k // 8, 1), owner]
-        else:
-            part = Gb.at[pl.ds(2 * k - 1, 2), owner]
+        part = Gb.at[k, owner]
         return remote(part, part, ssem, rsem, dev)
 
     def own_y(k):
@@ -164,8 +156,8 @@
     g_one.start()
     g_local.wait()
     g_sib.wait()
-    own_y(Single(0)).start()
-    start_own_x(Single(0))
+    own_y(0).start()
+    start_own_x(0)
     gram(rows_h, piece_a)
 
     def x_dev(j):
@@ -186,7 +178,7 @@
     G2[...] = GSG[yh] + RG1[...]
     for j in (2, 1, 3):
         g_two(j).start()
-    start_peer_x(Single(0))
+    start_peer_x(0)
     for j in range(1, 4):
         a_one(j).wait_recv()
     RA1[x] = GSA[x]
@@ -218,7 +210,7 @@
 
     for j in range(1, 8):
         sq_copy(j).start()
-    start_fwd_x(Single(0))
+    start_fwd_x(0)
     for k in range(1, 4):
         own_y(k).start()
     for j in range(1, 8):
@@ -358,18 +350,10 @@
     Pz[0, :, :, :, late] = jnp.zeros((4, 2, RW, MC - ZC), F32)
 
     def step(k, carry):
-        j = k // 2
-        even = k % 2 == 0
-
-        @pl.when((~even) & (k < PH - 1))
-        def _():
-            wait_rest(j + 1)
-
-        for p, now in ((0, 0), (8, PH - 1)):
-
-            @pl.when(k == now)
-            def _():
-                wait_rest(Single(p))
+
+        @pl.when(k < PH)
+        def _():
+            wait_rest(k)
 
         @pl.when((k >= SLOTS) & (k <= PH))
         def _():
@@ -406,19 +390,21 @@
             start_fwd_x(1)
             start_peer_x(2)
 
-        def at(when, op, ahead, last):
-            @pl.when(when & (j + ahead < GP - 1))
-            def _():
-                op(j + ahead)
-
-            @pl.when(k == last)
-            def _():
-                op(Single(GP - 1))
-
-        at(~even, start_fwd_x, 2, 13)
-        at(~even, start_peer_x, 3, 11)
-        at(even, start_own_x, 3, 10)
-        at(even, lambda p: own_y(p).start(), 4, 8)
+        @pl.when(k + 4 < PH)
+        def _():
+            own_y(k + 4).start()
+
+        @pl.when(k + 3 < PH)
+        def _():
+            start_own_x(k + 3)
+
+        @pl.when(k + 2 < PH)
+        def _():
+            start_fwd_x(k + 2)
+
+        @pl.when(k + 3 < PH)
+        def _():
+            start_peer_x(k + 3)
 
         @pl.when((k >= 2) & (k <= PH + 1))
         def _():
@@ -445,9 +431,7 @@
             fwd_x(k, d).wait_send()
         return carry
 
-    lax.fori_loop(1, GP - 1, drain, 0)
-    drain(Single(0), 0)
-    drain(Single(GP - 1), 0)
+    lax.fori_loop(0, PH, drain, 0)
     lax.fori_loop(PH - SLOTS + 1, PH, lambda k, carry: (free(k), carry)[1], 0)
     for kind in range(3):
         for d in range(2):
@@ -494,9 +478,9 @@
             dma((8,)),
             dma((8,)),
             dma((2,)),
-            dma((GP, 7)),
-            dma((GP, 2, 3)),
-            dma((GP,)),
+            dma((PH, 7)),
+            dma((PH, 2, 3)),
+            dma((PH,)),
             dma((SLOTS, 8)),
             dma((PH + 1, 2, 3)),
             dma((PH,)),

time: 164 us -> 159 us (0.970)
  Pallas kernels: 160 us -> 156 us
    pallas_call x1, Pallas kernels: 160 us -> 156 us  [per_device(): pl.pallas_call(kernel, out_shape=jax.ShapeDtypeStruct((256, FL), F32), in...]
where the time goes in v4:
time: 159 us
  Pallas kernels  156 us (98%)
  other arithmetic  2.94 us (2%)
    pallas_call x1, Pallas kernels, per_device(): pl.pallas_call(kernel, out_shape=jax.ShapeDtypeStruct((256, FL), F32), in...  156 us

profile of v4, /device:TPU:0, one launch (start us, length us, event | category | flops | bytes accessed | tf_op | source)
XLA Modules:
  0.0 159.1 jit_solution(14085972374336215180)
XLA Ops:
  0.0 0.0 copy-start
  0.0 156.1 %shard_map.37 = f32[256,1792]{1,0:T(8,128)} custom-call(bf16[1536,1792]{1,0:T(8,128)(2,1)} %act.1, bf16[1536,512]{1,0:T(8,128)(2,1)} %g.1), custom_call_target="tpu_custom_call" | custom-call | flops 24000000000 | bytes 9000000 | tf_op jit(solution)/shard_map/pallas_call | solution.py:444
  156.2 0.0 copy-done
  156.2 2.9 %add_multiply_fusion = f32[256,1792]{1,0:T(8,128)} fusion(f32[256,1792]{1,0:T(8,128)} %shard_map.37, f32[256,1792]{1,0:T(8,128)S(1)} %copy-done), kind=kLoop, calls=%fused_computation | loop fusion | flops 917504 | bytes 5505024 | tf_op jit(solution)/shard_map/div | solution.py:495
Async XLA Ops:
  0.0 156.2 %copy-start = (f32[256,1792]{1,0:T(8,128)S(1)}, f32[256,1792]{1,0:T(8,128)}, u32[]{:S(2)}) copy-start(f32[256,1792]{1,0:T(8,128)} %param.5) | copy-start | bytes 5505028

commit v5 on v4

--- a/solution.py
+++ b/solution.py
@@ -211,7 +211,7 @@
     for j in range(1, 8):
         sq_copy(j).start()
     start_fwd_x(0)
-    for k in range(1, 4):
+    for k in range(1, 5):
         own_y(k).start()
     for j in range(1, 8):
         sq_copy(j).wait_recv()
@@ -226,6 +226,8 @@
     fac_sib.start()
     start_peer_x(1)
     start_own_x(2)
+    for k in (5, 6):
+        own_y(k).start()
     h_sib.wait()
     fac_sib.wait()
     g_one.wait_send()
@@ -390,21 +392,21 @@
             start_fwd_x(1)
             start_peer_x(2)
 
-        @pl.when(k + 4 < PH)
-        def _():
-            own_y(k + 4).start()
+        @pl.when(k + 7 < PH)
+        def _():
+            own_y(k + 7).start()
 
         @pl.when(k + 3 < PH)
         def _():
             start_own_x(k + 3)
 
+        @pl.when(k + 3 < PH)
+        def _():
+            start_peer_x(k + 3)
+
         @pl.when(k + 2 < PH)
         def _():
             start_fwd_x(k + 2)
-
-        @pl.when(k + 3 < PH)
-        def _():
-            start_peer_x(k + 3)
 
         @pl.when((k >= 2) & (k <= PH + 1))
         def _():

time: 159 us -> 159 us (level)
  no operation moved by 1% of the time
where the time goes in v5:
time: 159 us
  Pallas kernels  156 us (98%)
  other arithmetic  2.94 us (2%)
    pallas_call x1, Pallas kernels, per_device(): pl.pallas_call(kernel, out_shape=jax.ShapeDtypeStruct((256, FL), F32), in...  156 us

profile of v5, /device:TPU:0, one launch (start us, length us, event | category | flops | bytes accessed | tf_op | source)
XLA Modules:
  0.0 158.9 jit_solution(7745585474972238942)
XLA Ops:
  0.0 0.0 copy-start
  0.0 156.0 %shard_map.37 = f32[256,1792]{1,0:T(8,128)} custom-call(bf16[1536,1792]{1,0:T(8,128)(2,1)} %act.1, bf16[1536,512]{1,0:T(8,128)(2,1)} %g.1), custom_call_target="tpu_custom_call" | custom-call | flops 24000000000 | bytes 9000000 | tf_op jit(solution)/shard_map/pallas_call | solution.py:446
  156.0 0.0 copy-done
  156.0 2.9 %add_multiply_fusion = f32[256,1792]{1,0:T(8,128)} fusion(f32[256,1792]{1,0:T(8,128)} %shard_map.37, f32[256,1792]{1,0:T(8,128)S(1)} %copy-done), kind=kLoop, calls=%fused_computation | loop fusion | flops 917504 | bytes 5505024 | tf_op jit(solution)/shard_map/div | solution.py:497
Async XLA Ops:
  0.0 156.0 %copy-start = (f32[256,1792]{1,0:T(8,128)S(1)}, f32[256,1792]{1,0:T(8,128)}, u32[]{:S(2)}) copy-start(f32[256,1792]{1,0:T(8,128)} %param.5) | copy-start | bytes 5505028

commit v6 on v5

--- a/solution.py
+++ b/solution.py
@@ -300,8 +300,8 @@
         y1_copy(k).wait_recv()
         Pz[(k + 1) % SLOTS, :, :, :, late] = Py[k % SLOTS, yl] + YZ[k]
 
-    def z_first(k, cols):
-        for kind in range(2):
+    def z_first(k, cols, kinds=(0, 1)):
+        for kind in kinds:
             for d in range(2):
                 z_copy(k, d, kind, cols).start()
 
@@ -373,7 +373,7 @@
 
         @pl.when(k < PH)
         def _():
-            z_first(k, slice(0, MC))
+            z_first(k, slice(0, MC), (0,))
 
         @pl.when(k == PH)
         def _():
@@ -382,6 +382,10 @@
         @pl.when((k >= 1) & (k <= PH))
         def _():
             z_relay(k - 1, slice(0, MC))
+
+        @pl.when(k < PH)
+        def _():
+            z_first(k, slice(0, MC), (1,))
 
         @pl.when(k == PH + 1)
         def _():

time: 159 us -> 159 us (level)
  no operation moved by 1% of the time
where the time goes in v6:
time: 159 us
  Pallas kernels  156 us (98%)
  other arithmetic  2.94 us (2%)
    pallas_call x1, Pallas kernels, per_device(): pl.pallas_call(kernel, out_shape=jax.ShapeDtypeStruct((256, FL), F32), in...  156 us

profile of v6, /device:TPU:0, one launch (start us, length us, event | category | flops | bytes accessed | tf_op | source)
XLA Modules:
  0.0 158.9 jit_solution(15582203078791735341)
XLA Ops:
  0.0 0.0 copy-start
  0.0 156.0 %shard_map.37 = f32[256,1792]{1,0:T(8,128)} custom-call(bf16[1536,1792]{1,0:T(8,128)(2,1)} %act.1, bf16[1536,512]{1,0:T(8,128)(2,1)} %g.1), custom_call_target="tpu_custom_call" | custom-call | flops 24000000000 | bytes 9000000 | tf_op jit(solution)/shard_map/pallas_call | solution.py:450
  156.0 0.0 copy-done
  156.0 2.9 %add_multiply_fusion = f32[256,1792]{1,0:T(8,128)} fusion(f32[256,1792]{1,0:T(8,128)} %shard_map.37, f32[256,1792]{1,0:T(8,128)S(1)} %copy-done), kind=kLoop, calls=%fused_computation | loop fusion | flops 917504 | bytes 5505024 | tf_op jit(solution)/shard_map/div | solution.py:501
Async XLA Ops:
  0.0 156.0 %copy-start = (f32[256,1792]{1,0:T(8,128)S(1)}, f32[256,1792]{1,0:T(8,128)}, u32[]{:S(2)}) copy-start(f32[256,1792]{1,0:T(8,128)} %param.5) | copy-start | bytes 5505028
